TPU v7x, 256 devices: a whole 4x4x8 slice. The times are simulated.
256 devices in a mesh: dp: 8 (over z), expert: 32 (over x, y, core).
Axes of the slice: x: 4, y: 4, z: 8, core: 2. Of those that a mesh axis runs over, the one named last changes fastest.
Arguments:
- tokens: bfloat16 [2048, 7168], P('expert', 'dp'), may hold values from -6 to 6
- tangent: bfloat16 [2048, 7168], P('expert', 'dp'), may hold values from -6 to 6
- cotangent: bfloat16 [2048, 7168], P('expert', 'dp'), may hold values from -3 to 3
- routing: int32 [2048, 8], P('expert'), may hold values from 0 to 31, all different within a row; in each aligned block of 64 rows (0 to 63, 64 to 127, ...) at most 18 rows name the same one
- gate_weights: float32 [2048, 8], P('expert'), may hold values from 0.1 to 0.6
- gate_proj: bfloat16 [32, 7168, 2048], P('expert', 'dp'), may hold values from -0.0625 to 0.0625
- up_proj: bfloat16 [32, 7168, 2048], P('expert', 'dp'), may hold values from -0.0625 to 0.0625
- down_proj: bfloat16 [32, 2048, 7168], P('expert', None, 'dp'), may hold values from -0.125 to 0.125
Outputs:
- hessian_product: float32 [2048, 7168], P('expert', 'dp')
Inputs may be any that keep to these rules, and one draw needn't show every extreme that they name: `routing`: each token names 8 different experts. In each aligned block of 64 tokens (the tokens of one index of expert) no expert is named more than 18 times, a bound that some block reaches.
All inputs are finite; a program needn't handle non-finite values.
Results may differ from a plain program's by a relative error of at most 0.0041.
Values may be sent and summed in bfloat16 or wider, within the bound.
A program may use at most 128 MiB of HBM per device.

v0:
```python
import jax
import jax.numpy as jnp
from jax import lax
from jax.sharding import PartitionSpec as P

TOP = 8


def second_order(pre_gate, pre_up, tangent_gate, tangent_up, back_hidden):
    sigma = jax.nn.sigmoid(pre_gate)
    first_slope = sigma * (1.0 + pre_gate * (1.0 - sigma))
    second_slope = sigma * (1.0 - sigma) * (2.0 + pre_gate * (1.0 - 2.0 * sigma))
    factor_a = back_hidden * (second_slope * tangent_gate * pre_up + first_slope * tangent_up)
    factor_b = back_hidden * first_slope * tangent_gate
    return (factor_a.astype(jnp.bfloat16), factor_b.astype(jnp.bfloat16))


def contract_last(left_rows, right_matrix):
    return lax.dot_general(
        left_rows, right_matrix, (((1,), (1,)), ((), ())), preferred_element_type=jnp.float32
    )


def shards(tokens, tangent, cotangent, routing, gate_weights, gate_proj, up_proj, down_proj):
    expert_count = lax.axis_size("expert")
    tok_rows = tokens.shape[0]
    feat_cols = tokens.shape[1]
    capacity = min(tok_rows, tok_rows * TOP // expert_count * 9 // 8)
    slot_total = expert_count * capacity
    routed_flat = routing.reshape(-1)
    route_hits = (
        routed_flat[:, None] == jnp.arange(expert_count, dtype=jnp.int32)[None, :]
    ).astype(jnp.int32)
    slot_index = jnp.sum((jnp.cumsum(route_hits, axis=0) - route_hits) * route_hits, axis=1)
    target_row = routed_flat * capacity + slot_index

    def scatter_rows(values):
        spread = jnp.repeat(values, TOP, axis=0)
        zero_buf = jnp.zeros((slot_total, values.shape[1]), values.dtype)
        return zero_buf.at[target_row].set(spread).reshape(expert_count, capacity, values.shape[1])

    x_rows = lax.all_to_all(
        scatter_rows(tokens), "expert", split_axis=0, concat_axis=0, tiled=True
    ).reshape(slot_total, feat_cols)
    paired = jnp.concatenate([tangent, cotangent], axis=1)
    paired_rows = lax.all_to_all(
        scatter_rows(paired), "expert", split_axis=0, concat_axis=0, tiled=True
    ).reshape(slot_total, 2 * feat_cols)
    v_rows = paired_rows[:, :feat_cols]
    c_rows = paired_rows[:, feat_cols:]
    gate_cols = gate_proj[0]
    up_cols = up_proj[0]
    down_rows = down_proj[0]
    part_gate = jnp.dot(x_rows, gate_cols, preferred_element_type=jnp.float32)
    part_up = jnp.dot(x_rows, up_cols, preferred_element_type=jnp.float32)
    part_tgate = jnp.dot(v_rows, gate_cols, preferred_element_type=jnp.float32)
    part_tup = jnp.dot(v_rows, up_cols, preferred_element_type=jnp.float32)
    part_back = contract_last(c_rows, down_rows)
    summed = (
        lax.psum_scatter(part_gate, "dp", scatter_dimension=0, tiled=True),
        lax.psum_scatter(part_up, "dp", scatter_dimension=0, tiled=True),
        lax.psum_scatter(part_tgate, "dp", scatter_dimension=0, tiled=True),
        lax.psum_scatter(part_tup, "dp", scatter_dimension=0, tiled=True),
        lax.psum_scatter(part_back, "dp", scatter_dimension=0, tiled=True),
    )
    factor_a, factor_b = second_order(summed[0], summed[1], summed[2], summed[3], summed[4])
    factors = jnp.stack([factor_a, factor_b])
    piece = lax.all_gather(factors, "dp", axis=1, tiled=True)
    result_rows = contract_last(piece[0], gate_cols) + contract_last(piece[1], up_cols)
    outgoing = result_rows.astype(jnp.bfloat16).reshape(expert_count, capacity, feat_cols)
    returned = lax.all_to_all(outgoing, "expert", split_axis=0, concat_axis=0, tiled=True).reshape(
        slot_total, feat_cols
    )
    gathered = returned[target_row].reshape(tok_rows, TOP, feat_cols).astype(jnp.float32)
    return jnp.sum(gate_weights[:, :, None] * gathered, axis=1)


def solution(mesh):
    in_specs = (
        P("expert", "dp"),
        P("expert", "dp"),
        P("expert", "dp"),
        P("expert", None),
        P("expert", None),
        P("expert", "dp", None),
        P("expert", "dp", None),
        P("expert", None, "dp"),
    )
    out_specs = P("expert", "dp")
    return jax.shard_map(shards, mesh=mesh, in_specs=in_specs, out_specs=out_specs, check_vma=False)
```

profile of v0, /device:TPU:1, one launch (start us, length us, event | category | flops | bytes accessed | tf_op | source)
XLA Modules:
  0.0 463.8 jit_solution(245255507557251218)
XLA Ops:
  6.5 0.8 copy.12
  7.3 0.1 eq.29
  7.4 0.1 eq.25
  7.5 0.7 broadcast_multiply_fusion
  8.2 1.2 reduce-window.6
  9.4 0.2 slice_reduce_fusion
  9.7 0.1 copy.11
  9.7 0.1 mul.66
  9.8 0.1 fusion.40
  10.0 3.0 scatter_custom_fusion.1
  12.9 0.3 reshape.79
  13.3 29.3 %all_to_all.15 = bf16[32,18,896]{2,1,0:T(8,128)(2,1)S(1)} all-to-all(bf16[32,18,896]{2,1,0:T(8,128)(2,1)S(1)} %reshape.79), channel_id=1, replica_groups=mesh['dp'=8,'expert'=32] {'expert'}, dimensions={0} | all-to-all | bytes 2064384 | tf_op jit(solution)/shard_map/all_to_all | solution.py:42
  42.6 0.3 reshape.80
  42.9 6.3 %fusion.4 = f32[576,2048]{1,0:T(8,128)} fusion(bf16[576,896]{1,0:T(8,128)(2,1)S(1)} %reshape.80, bf16[1,896,2048]{2,1,0:T(8,128)(2,1)} %param.14), kind=kOutput, calls=%fused_computation.7 | convolution fusion | flops 2113929216 | bytes 9420800 | tf_op jit(solution)/shard_map/dot_general | solution.py:55
  49.2 0.0 reduce-scatter.12.cloned.1.call-update
  49.2 0.0 reduce-scatter.8.cloned.1.call-start
  49.3 6.3 %fusion.10 = f32[576,2048]{1,0:T(8,128)} fusion(bf16[576,896]{1,0:T(8,128)(2,1)S(1)} %reshape.80, bf16[1,896,2048]{2,1,0:T(8,128)(2,1)} %param.13), kind=kOutput, calls=%fused_computation.13 | convolution fusion | flops 2113929216 | bytes 9420800 | tf_op jit(solution)/shard_map/dot_general | solution.py:54
  55.6 0.0 reduce-scatter.10.cloned.1.call-start
  55.7 0.8 copy-done.1
  56.5 0.1 copy-done.2
  56.6 4.8 %scatter_custom_fusion = bf16[576,1792]{1,0:T(8,128)(2,1)} fusion(s32[512]{0:T(512)S(1)} %bitcast.64, bf16[]{:T(256)} %constant.7.clone.1, bf16[64,1792]{1,0:T(8,128)(2,1)S(1)} %pad_maximum_fusion.1), kind=kCustom, calls=%fused_computation.22 | custom fusion | bytes 2293762 | tf_op jit(solution)/shard_map/scatter | solution.py:40
  61.4 2.6 reshape.76
  64.0 39.1 %all_to_all.16 = bf16[32,18,1792]{2,1,0:T(8,128)(2,1)} all-to-all(bf16[32,18,1792]{2,1,0:T(8,128)(2,1)S(1)} %reshape.76), channel_id=1, replica_groups=mesh['dp'=8,'expert'=32] {'expert'}, dimensions={0} | all-to-all | bytes 4128768 | tf_op jit(solution)/shard_map/all_to_all | solution.py:46
  103.1 2.8 reshape.77
  105.9 6.4 %fusion.8 = f32[576,2048]{1,0:T(8,128)} fusion(bf16[1,896,2048]{2,1,0:T(8,128)(2,1)} %param.13, bf16[576,1792]{1,0:T(8,128)(2,1)S(1)} %reshape.77), kind=kOutput, calls=%fused_computation.11 | convolution fusion | flops 2113929216 | bytes 9420800 | tf_op jit(solution)/shard_map/dot_general | solution.py:56
  112.3 0.0 reduce-scatter.10.cloned.1.call-update
  112.3 0.2 reduce-scatter.14.cloned.1.call-start
  112.6 6.3 %fusion.2 = f32[576,2048]{1,0:T(8,128)} fusion(bf16[1,896,2048]{2,1,0:T(8,128)(2,1)} %param.14, bf16[576,1792]{1,0:T(8,128)(2,1)S(1)} %reshape.77), kind=kOutput, calls=%fused_computation.5 | convolution fusion | flops 2113929216 | bytes 9420800 | tf_op jit(solution)/shard_map/dot_general | solution.py:57
  118.9 0.0 reduce-scatter.6.cloned.1.call-start
  118.9 6.4 %fusion.12 = f32[576,2048]{1,0:T(8,128)} fusion(bf16[1,2048,896]{2,1,0:T(8,128)(2,1)} %param.15, bf16[576,1792]{1,0:T(8,128)(2,1)S(1)} %reshape.77), kind=kOutput, calls=%fused_computation.15 | convolution fusion | flops 2113929216 | bytes 9420800 | tf_op jit(solution)/shard_map/dot_general | solution.py:19
  125.3 0.0 all-gather.2.cloned.1.call-start
  125.4 0.0 reduce-scatter.12.cloned.1.call-done
  125.4 44.6 %reduce-scatter.8.cloned.1.call-done = f32[72,2048]{1,0:T(8,128)} async-done(((f32[576,2048]{1,0:T(8,128)}), f32[72,2048]{1,0:T(8,128)}) %reduce-scatter.8.cloned.1.call-update) | async-done | bytes 589840 | tf_op jit(solution)/shard_map/reduce_scatter | solution.py:60
  170.0 61.5 %reduce-scatter.10.cloned.1.call-done = f32[72,2048]{1,0:T(8,128)} async-done(((f32[576,2048]{1,0:T(8,128)}), f32[72,2048]{1,0:T(8,128)}) %reduce-scatter.10.cloned.1.call-update) | async-done | bytes 589840 | tf_op jit(solution)/shard_map/reduce_scatter | solution.py:62
  231.5 61.3 %reduce-scatter.14.cloned.1.call-done = f32[72,2048]{1,0:T(8,128)} async-done(((f32[576,2048]{1,0:T(8,128)}), f32[72,2048]{1,0:T(8,128)}) %reduce-scatter.14.cloned.1.call-update) | async-done | bytes 589840 | tf_op jit(solution)/shard_map/reduce_scatter | solution.py:63
  292.8 61.3 %reduce-scatter.6.cloned.1.call-done = f32[72,2048]{1,0:T(8,128)} async-done(((f32[576,2048]{1,0:T(8,128)}), f32[72,2048]{1,0:T(8,128)}) %reduce-scatter.6.cloned.1.call-update) | async-done | bytes 589840 | tf_op jit(solution)/shard_map/reduce_scatter | solution.py:64
  354.1 2.2 fusion.37
  356.3 0.9 pad_maximum_fusion
  357.2 58.5 %all-gather.2.cloned.1.call-done = bf16[2,576,2048]{2,1,0:T(8,128)(2,1)} async-done(((bf16[2,72,2048]{2,1,0:T(8,128)(2,1)}), bf16[2,576,2048]{2,1,0:T(8,128)(2,1)}) %all-gather.2.cloned.1.call-update) | async-done | bytes 4718608 | tf_op jit(solution)/shard_map/all_gather | solution.py:68
  415.7 5.5 %fusion = f32[576,896]{1,0:T(8,128)S(1)} fusion(bf16[1,896,2048]{2,1,0:T(8,128)(2,1)} %param.14, bf16[2,576,2048]{2,1,0:T(8,128)(2,1)} %all-gather.2.cloned.1.call-done), kind=kOutput, calls=%fused_computation.3 | convolution fusion | flops 2113929216 | bytes 8093696 | tf_op jit(solution)/shard_map/dot_general | solution.py:19
  421.3 2.7 add_convert_fusion
  423.9 1.3 reshape.81
  425.2 7.5 %all-to-all-start.2 = ((bf16[32,18,896]{2,1,0:T(8,128)(2,1)}), bf16[32,18,896]{2,1,0:T(8,128)(2,1)S(1)}, u32[]{:S(2)}, u32[]{:S(2)}) async-start(bf16[32,18,896]{2,1,0:T(8,128)(2,1)} %reshape.81), calls=%async_computation.7 | async-start | bytes 2752512 | tf_op jit(solution)/shard_map/all_to_all | solution.py:71
  432.7 0.1 copy.10
  432.8 20.4 %all-to-all-done.2 = bf16[32,18,896]{2,1,0:T(8,128)(2,1)S(1)} async-done(((bf16[32,18,896]{2,1,0:T(8,128)(2,1)}), bf16[32,18,896]{2,1,0:T(8,128)(2,1)S(1)}, u32[]{:S(2)}, u32[]{:S(2)}) %all-to-all-start.2) | async-done | bytes 1032224 | tf_op jit(solution)/shard_map/all_to_all | solution.py:71
  453.2 0.3 reshape.82
  453.6 2.1 gather_fusion
  455.6 1.3 fusion.14
  (21 shorter events, 0.2 us)
Async XLA Ops:
  6.5 3.4 copy-start
  6.5 118.8 %reduce-scatter.12.cloned.1.call-start = ((), (), s32[]{:S(2)}) async-start(), calls=%async_computation.11 | async-start | bytes 5308416 | tf_op jit(solution)/shard_map/reduce_scatter | solution.py:61
  49.2 120.8 %reduce-scatter.8.cloned.1.call-start = ((), (), s32[]{:S(2)}) async-start(), calls=%async_computation.9 | async-start | bytes 5308416 | tf_op jit(solution)/shard_map/reduce_scatter | solution.py:60
  55.6 0.9 copy-start.1
  55.6 1.0 copy-start.2
  55.6 175.8 %reduce-scatter.10.cloned.1.call-start = ((), (), s32[]{:S(2)}) async-start(), calls=%async_computation.10 | async-start | bytes 5308416 | tf_op jit(solution)/shard_map/reduce_scatter | solution.py:62
  112.3 180.5 %reduce-scatter.14.cloned.1.call-start = ((), (), s32[]{:S(2)}) async-start(), calls=%async_computation.12 | async-start | bytes 5308416 | tf_op jit(solution)/shard_map/reduce_scatter | solution.py:63
  118.9 235.2 %reduce-scatter.6.cloned.1.call-start = ((), (), s32[]{:S(2)}) async-start(), calls=%async_computation.8 | async-start | bytes 5308416 | tf_op jit(solution)/shard_map/reduce_scatter | solution.py:64
  125.3 290.4 %all-gather.2.cloned.1.call-start = ((), (), s32[]{:S(2)}) async-start(), calls=%async_computation.13 | async-start | bytes 5308416 | tf_op jit(solution)/shard_map/all_gather | solution.py:68
  415.7 5.5 %copy-start.4 = (bf16[2,576,2048]{2,1,0:T(8,128)(2,1)S(1)}, bf16[2,576,2048]{2,1,0:T(8,128)(2,1)}, u32[]{:S(2)}) copy-start(bf16[2,576,2048]{2,1,0:T(8,128)(2,1)} %all-gather.2.cloned.1.call-done) | copy-start | bytes 14155780
  415.7 5.5 %copy-start.5 = (bf16[1,896,2048]{2,1,0:T(8,128)(2,1)S(1)}, bf16[1,896,2048]{2,1,0:T(8,128)(2,1)}, u32[]{:S(2)}) copy-start(bf16[1,896,2048]{2,1,0:T(8,128)(2,1)} %param.13) | copy-start | bytes 11010052
  423.9 8.8 %copy-start.3 = (f32[64,8]{0,1:T(8,128)S(1)}, f32[64,8]{0,1:T(8,128)}, u32[]{:S(2)}) copy-start(f32[64,8]{0,1:T(8,128)} %param.12) | copy-start | bytes 6148
  425.2 28.0 %all-to-all-start.2 = ((bf16[32,18,896]{2,1,0:T(8,128)(2,1)}), bf16[32,18,896]{2,1,0:T(8,128)(2,1)S(1)}, u32[]{:S(2)}, u32[]{:S(2)}) async-start(bf16[32,18,896]{2,1,0:T(8,128)(2,1)} %reshape.81), calls=%async_computation.7 | async-start | bytes 2752512 | tf_op jit(solution)/shard_map/all_to_all | solution.py:71
Sparse Core Ops, SparseCore 0:
  49.3 59.1 reduce-scatter.11
  111.0 58.8 reduce-scatter.7
  172.5 58.8 reduce-scatter.9
  233.9 58.8 reduce-scatter.13
  295.2 58.8 reduce-scatter.5
  357.3 58.3 all-gather.1
where the time goes:
time: 464 us
  waiting for transfers between devices  308 us (66%)
  blocking collectives  68.4 us (15%)
  matrix products  39.8 us (9%)
  local copies, waits for them, and re-layouts  19.9 us (4%)
  between operations  13.6 us (3%)
  starting transfers between devices  7.92 us (2%)
  other arithmetic  6.42 us (1%)
    reduce_scatter x1, waiting for transfers between devices, shards(): lax.psum_scatter(part_tgate, 'dp', scatter_dimension=0, tiled=True)  61.5 us
    reduce_scatter x1, waiting for transfers between devices, shards(): lax.psum_scatter(part_tup, 'dp', scatter_dimension=0, tiled=True)  61.3 us
    reduce_scatter x1, waiting for transfers between devices, shards(): lax.psum_scatter(part_back, 'dp', scatter_dimension=0, tiled=True)  61.3 us
    all_gather x1, waiting for transfers between devices, shards(): piece = lax.all_gather(factors, 'dp', axis=1, tiled=True)  58.5 us
    reduce_scatter x1, waiting for transfers between devices, shards(): lax.psum_scatter(part_gate, 'dp', scatter_dimension=0, tiled=True)  44.6 us
    all_to_all x1, blocking collectives, shards(): lax.all_to_all(scatter_rows(paired), 'expert', split_axis=0, concat_axis=...  39.1 us
    all_to_all x1, blocking collectives, shards(): lax.all_to_all(scatter_rows(tokens), 'expert', split_axis=0, concat_axis=...  29.3 us
    all_to_all x1, waiting for transfers between devices, shards(): lax.all_to_all(outgoing, 'expert', split_axis=0, concat_axis=0, tiled=True)  20.4 us
  transfers between devices with their start and end apart: 7, of which 6 were waited for; matrix products, arithmetic and copies ran while one was open for 8% of the time, Pallas kernels for 0%

commit v1 on v0

--- a/solution.py
+++ b/solution.py
@@ -1,9 +1,19 @@
+import functools
 import jax
 import jax.numpy as jnp
 from jax import lax
 from jax.sharding import PartitionSpec as P
 
 TOP = 8
+
+
+def do_samples_all(block_here, k_dim):
+    work_now = jnp.stack([block_here for _ in range(lax.axis_size("dp"))])
+    passed = lax.all_to_all(work_now, "dp", split_axis=0, concat_axis=0)
+    return jnp.concatenate(passed, k_dim)
+
+
+tokens_feed = functools.partial(do_samples_all, k_dim=1)
 
 
 def second_order(pre_gate, pre_up, tangent_gate, tangent_up, back_hidden):
@@ -65,7 +75,7 @@
     )
     factor_a, factor_b = second_order(summed[0], summed[1], summed[2], summed[3], summed[4])
     factors = jnp.stack([factor_a, factor_b])
-    piece = lax.all_gather(factors, "dp", axis=1, tiled=True)
+    piece = tokens_feed(factors)
     result_rows = contract_last(piece[0], gate_cols) + contract_last(piece[1], up_cols)
     outgoing = result_rows.astype(jnp.bfloat16).reshape(expert_count, capacity, feat_cols)
     returned = lax.all_to_all(outgoing, "expert", split_axis=0, concat_axis=0, tiled=True).reshape(

time: 464 us -> 516 us (1.11)
  blocking collectives: 68.4 us -> 178 us
  waiting for transfers between devices: 308 us -> 249 us
    all_to_all x0 -> x1, blocking collectives: none -> 110 us  [do_samples_all(): passed = lax.all_to_all(work_now, 'dp', split_axis=0, concat_axis=0)]
    all_gather x1 -> x0, waiting for transfers between devices: 58.5 us -> none  [shards(): piece = lax.all_gather(factors, 'dp', axis=1, tiled=True)]
  transfers between devices with their start and end apart: 7 -> 6, of which waited for: 6 -> 5; matrix products, arithmetic and copies ran while one was open for 8% -> 7% of each run, Pallas kernels for 0% -> 0%
where the time goes in v1:
time: 516 us; the launch traced here: 515 us
  waiting for transfers between devices  249 us (48%)
  blocking collectives  178 us (34%)
  matrix products  36.9 us (7%)
  local copies, waits for them, and re-layouts  22.5 us (4%)
  between operations  13.3 us (3%)
  starting transfers between devices  9.55 us (2%)
  other arithmetic  5.59 us (1%)
    all_to_all x1, blocking collectives, do_samples_all(): passed = lax.all_to_all(work_now, 'dp', split_axis=0, concat_axis=0)  110 us
    reduce_scatter x1, waiting for transfers between devices, shards(): lax.psum_scatter(part_tgate, 'dp', scatter_dimension=0, tiled=True)  61.5 us
    reduce_scatter x1, waiting for transfers between devices, shards(): lax.psum_scatter(part_back, 'dp', scatter_dimension=0, tiled=True)  61.3 us
    reduce_scatter x1, waiting for transfers between devices, shards(): lax.psum_scatter(part_tup, 'dp', scatter_dimension=0, tiled=True)  61.3 us
    reduce_scatter x1, waiting for transfers between devices, shards(): lax.psum_scatter(part_gate, 'dp', scatter_dimension=0, tiled=True)  44.6 us
    all_to_all x1, blocking collectives, shards(): lax.all_to_all(scatter_rows(paired), 'expert', split_axis=0, concat_axis=...  39.1 us
    all_to_all x1, blocking collectives, shards(): lax.all_to_all(scatter_rows(tokens), 'expert', split_axis=0, concat_axis=...  29.3 us
    all_to_all x1, waiting for transfers between devices, shards(): lax.all_to_all(outgoing, 'expert', split_axis=0, concat_axis=0, tiled=True)  20.4 us
  transfers between devices with their start and end apart: 6, of which 5 were waited for; matrix products, arithmetic and copies ran while one was open for 7% of the time, Pallas kernels for 0%

profile of v1, /device:TPU:1, one launch (start us, length us, event | category | flops | bytes accessed | tf_op | source)
XLA Modules:
  0.0 515.4 jit_solution(7727833547130050697)
XLA Ops:
  6.5 0.8 copy.12
  7.3 0.1 eq.29
  7.4 0.1 eq.25
  7.5 0.7 broadcast_multiply_fusion
  8.2 1.2 reduce-window.6
  9.4 0.2 slice_reduce_fusion
  9.7 0.1 copy.11
  9.7 0.1 mul.66
  9.8 0.1 fusion.40
  10.0 3.0 scatter_custom_fusion.1
  12.9 0.3 reshape.89
  13.3 29.3 %all_to_all.20 = bf16[32,18,896]{2,1,0:T(8,128)(2,1)S(1)} all-to-all(bf16[32,18,896]{2,1,0:T(8,128)(2,1)S(1)} %reshape.89), channel_id=1, replica_groups=mesh['dp'=8,'expert'=32] {'expert'}, dimensions={0} | all-to-all | bytes 2064384 | tf_op jit(solution)/shard_map/all_to_all | solution.py:52
  42.6 0.3 reshape.90
  42.9 6.3 %fusion.4 = f32[576,2048]{1,0:T(8,128)} fusion(bf16[576,896]{1,0:T(8,128)(2,1)S(1)} %reshape.90, bf16[1,896,2048]{2,1,0:T(8,128)(2,1)} %param.14), kind=kOutput, calls=%fused_computation.7 | convolution fusion | flops 2113929216 | bytes 9420800 | tf_op jit(solution)/shard_map/dot_general | solution.py:65
  49.2 0.0 reduce-scatter.8.cloned.1.call-start
  49.3 6.3 %fusion.10 = f32[576,2048]{1,0:T(8,128)} fusion(bf16[576,896]{1,0:T(8,128)(2,1)S(1)} %reshape.90, bf16[1,896,2048]{2,1,0:T(8,128)(2,1)} %param.13), kind=kOutput, calls=%fused_computation.13 | convolution fusion | flops 2113929216 | bytes 9420800 | tf_op jit(solution)/shard_map/dot_general | solution.py:64
  55.6 0.0 reduce-scatter.10.cloned.1.call-start
  55.7 0.8 copy-done.2
  56.5 0.1 copy-done.3
  56.6 4.8 scatter_custom_fusion
  61.4 2.6 reshape.86
  64.0 39.1 %all_to_all.21 = bf16[32,18,1792]{2,1,0:T(8,128)(2,1)} all-to-all(bf16[32,18,1792]{2,1,0:T(8,128)(2,1)S(1)} %reshape.86), channel_id=1, replica_groups=mesh['dp'=8,'expert'=32] {'expert'}, dimensions={0} | all-to-all | bytes 4128768 | tf_op jit(solution)/shard_map/all_to_all | solution.py:56
  103.1 2.8 reshape.87
  105.9 6.4 %fusion.8 = f32[576,2048]{1,0:T(8,128)} fusion(bf16[1,896,2048]{2,1,0:T(8,128)(2,1)} %param.13, bf16[576,1792]{1,0:T(8,128)(2,1)S(1)} %reshape.87), kind=kOutput, calls=%fused_computation.11 | convolution fusion | flops 2113929216 | bytes 9420800 | tf_op jit(solution)/shard_map/dot_general | solution.py:66
  112.3 0.2 reduce-scatter.14.cloned.1.call-start
  112.6 6.3 %fusion.2 = f32[576,2048]{1,0:T(8,128)} fusion(bf16[1,896,2048]{2,1,0:T(8,128)(2,1)} %param.14, bf16[576,1792]{1,0:T(8,128)(2,1)S(1)} %reshape.87), kind=kOutput, calls=%fused_computation.5 | convolution fusion | flops 2113929216 | bytes 9420800 | tf_op jit(solution)/shard_map/dot_general | solution.py:67
  118.9 0.0 reduce-scatter.6.cloned.1.call-start
  118.9 6.4 %fusion.12 = f32[576,2048]{1,0:T(8,128)} fusion(bf16[1,2048,896]{2,1,0:T(8,128)(2,1)} %param.15, bf16[576,1792]{1,0:T(8,128)(2,1)S(1)} %reshape.87), kind=kOutput, calls=%fused_computation.15 | convolution fusion | flops 2113929216 | bytes 9420800 | tf_op jit(solution)/shard_map/dot_general | solution.py:29
  125.3 0.0 reduce-scatter.12.cloned.1.call-done
  125.3 44.6 %reduce-scatter.8.cloned.1.call-done = f32[72,2048]{1,0:T(8,128)} async-done(((f32[576,2048]{1,0:T(8,128)}), f32[72,2048]{1,0:T(8,128)}) %reduce-scatter.8.cloned.1.call-update) | async-done | bytes 589840 | tf_op jit(solution)/shard_map/reduce_scatter | solution.py:70
  170.0 61.5 %reduce-scatter.10.cloned.1.call-done = f32[72,2048]{1,0:T(8,128)} async-done(((f32[576,2048]{1,0:T(8,128)}), f32[72,2048]{1,0:T(8,128)}) %reduce-scatter.10.cloned.1.call-update) | async-done | bytes 589840 | tf_op jit(solution)/shard_map/reduce_scatter | solution.py:72
  231.5 61.3 %reduce-scatter.14.cloned.1.call-done = f32[72,2048]{1,0:T(8,128)} async-done(((f32[576,2048]{1,0:T(8,128)}), f32[72,2048]{1,0:T(8,128)}) %reduce-scatter.14.cloned.1.call-update) | async-done | bytes 589840 | tf_op jit(solution)/shard_map/reduce_scatter | solution.py:73
  292.8 61.3 %reduce-scatter.6.cloned.1.call-done = f32[72,2048]{1,0:T(8,128)} async-done(((f32[576,2048]{1,0:T(8,128)}), f32[72,2048]{1,0:T(8,128)}) %reduce-scatter.6.cloned.1.call-update) | async-done | bytes 589840 | tf_op jit(solution)/shard_map/reduce_scatter | solution.py:74
  354.1 2.2 fusion.37
  356.3 0.1 pad_maximum_fusion
  356.4 0.6 stack.11
  357.0 109.8 %all_to_all.22 = bf16[8,2,72,2048]{3,2,1,0:T(8,128)(2,1)S(1)} all-to-all(bf16[8,2,72,2048]{3,2,1,0:T(8,128)(2,1)S(1)} %stack.11), channel_id=1, replica_groups=mesh['dp'=8,'expert'=32] {'dp'}, dimensions={0} | all-to-all | bytes 9437184 | tf_op jit(solution)/shard_map/all_to_all | solution.py:12
  466.8 0.7 fusion.42
  467.5 1.3 copy-done.5
  468.9 2.6 fusion
  471.5 2.7 add_convert_fusion
  474.2 1.3 reshape.92
  475.4 9.2 %all-to-all-start.3 = ((bf16[32,18,896]{2,1,0:T(8,128)(2,1)}), bf16[32,18,896]{2,1,0:T(8,128)(2,1)S(1)}, u32[]{:S(2)}, u32[]{:S(2)}) async-start(bf16[32,18,896]{2,1,0:T(8,128)(2,1)} %reshape.92), calls=%async_computation.8 | async-start | bytes 2752512 | tf_op jit(solution)/shard_map/all_to_all | solution.py:81
  484.7 0.1 copy.10
  484.8 20.4 %all-to-all-done.3 = bf16[32,18,896]{2,1,0:T(8,128)(2,1)S(1)} async-done(((bf16[32,18,896]{2,1,0:T(8,128)(2,1)}), bf16[32,18,896]{2,1,0:T(8,128)(2,1)S(1)}, u32[]{:S(2)}, u32[]{:S(2)}) %all-to-all-start.3) | async-done | bytes 1032224 | tf_op jit(solution)/shard_map/all_to_all | solution.py:81
  505.2 0.3 reshape.93
  505.5 2.1 gather_fusion
  507.6 1.3 fusion.14
  (23 shorter events, 0.2 us)
Async XLA Ops:
  6.5 3.4 copy-start
  6.5 118.8 %reduce-scatter.12.cloned.1.call-start = ((), (), s32[]{:S(2)}) async-start(), calls=%async_computation.12 | async-start | bytes 5308416 | tf_op jit(solution)/shard_map/reduce_scatter | solution.py:71
  49.2 120.8 %reduce-scatter.8.cloned.1.call-start = ((), (), s32[]{:S(2)}) async-start(), calls=%async_computation.10 | async-start | bytes 5308416 | tf_op jit(solution)/shard_map/reduce_scatter | solution.py:70
  55.6 0.9 copy-start.2
  55.6 1.0 copy-start.3
  55.6 175.8 %reduce-scatter.10.cloned.1.call-start = ((), (), s32[]{:S(2)}) async-start(), calls=%async_computation.11 | async-start | bytes 5308416 | tf_op jit(solution)/shard_map/reduce_scatter | solution.py:72
  112.3 180.4 %reduce-scatter.14.cloned.1.call-start = ((), (), s32[]{:S(2)}) async-start(), calls=%async_computation.13 | async-start | bytes 5308416 | tf_op jit(solution)/shard_map/reduce_scatter | solution.py:73
  118.9 235.2 %reduce-scatter.6.cloned.1.call-start = ((), (), s32[]{:S(2)}) async-start(), calls=%async_computation.9 | async-start | bytes 5308416 | tf_op jit(solution)/shard_map/reduce_scatter | solution.py:74
  466.8 2.0 copy-start.5
  468.9 2.6 copy-start.6
  474.2 10.5 %copy-start.4 = (f32[64,8]{0,1:T(8,128)S(1)}, f32[64,8]{0,1:T(8,128)}, u32[]{:S(2)}) copy-start(f32[64,8]{0,1:T(8,128)} %param.12) | copy-start | bytes 6148
  475.4 29.7 %all-to-all-start.3 = ((bf16[32,18,896]{2,1,0:T(8,128)(2,1)}), bf16[32,18,896]{2,1,0:T(8,128)(2,1)S(1)}, u32[]{:S(2)}, u32[]{:S(2)}) async-start(bf16[32,18,896]{2,1,0:T(8,128)(2,1)} %reshape.92), calls=%async_computation.8 | async-start | bytes 2752512 | tf_op jit(solution)/shard_map/all_to_all | solution.py:81
  505.5 3.4 copy-start.1
Sparse Core Ops, SparseCore 0:
  49.3 59.1 reduce-scatter.11
  111.0 58.8 reduce-scatter.7
  172.5 58.8 reduce-scatter.9
  233.9 58.8 reduce-scatter.13
  295.2 58.8 reduce-scatter.5
